TPU v7x, 128 devices: a whole 4x4x4 slice. The times are simulated.
128 devices in a mesh: dp: 8 (over y, core), seq: 16 (over x, z).
Axes of the slice: x: 4, y: 4, z: 4, core: 2. Of those that a mesh axis runs over, the one named last changes fastest.
Arguments:
- query: bfloat16 [8, 2048, 1536], P('dp', 'seq'), may hold values from -6 to 6
- key_in: bfloat16 [8, 2048, 1536], P('dp', 'seq'), may hold values from -6 to 6
- value: bfloat16 [8, 2048, 1536], P('dp', 'seq'), may hold values from -6 to 6
- grad_out: bfloat16 [8, 2048, 1536], P('dp', 'seq'), may hold values from -6 to 6
- expert_ids: int32 [8, 2048, 2], P('dp', 'seq'), may hold values from 0 to 15, all different within a row; in each aligned block of 128 rows (0 to 127, 128 to 255, ..., all dimensions but the last counted through in order) at most 18 rows name the same one
- gate_weights: float32 [8, 2048, 2], P('dp', 'seq'), may hold values from 0.25 to 1
- w_gate: bfloat16 [16, 1536, 4096], P('seq', None, 'dp'), may hold values from -0.15625 to 0.15625
- w_up: bfloat16 [16, 1536, 4096], P('seq', None, 'dp'), may hold values from -0.15625 to 0.15625
- w_down: bfloat16 [16, 4096, 1536], P('seq', 'dp'), may hold values from -0.09375 to 0.09375
Outputs:
- grad_query: bfloat16 [8, 2048, 1536], P('dp', 'seq')
- grad_key: bfloat16 [8, 2048, 1536], P('dp', 'seq')
- grad_value: bfloat16 [8, 2048, 1536], P('dp', 'seq')
- grad_down: bfloat16 [16, 4096, 1536], P('seq', 'dp')
Inputs may be any that keep to these rules, and one draw needn't show every extreme that they name: `expert_ids`: each token names two different experts; among the 128 tokens of one device no expert is named more than 18 times, and in every draw some expert is named exactly 18 times by some device.
All inputs are finite; a program needn't handle non-finite values.
Results may differ from a plain program's by a relative error of at most 0.024.
Values may be sent and summed in bfloat16 or wider, within the bound.
A program may use at most 192 MiB of HBM per device.

v0:
```python
import jax
import jax.numpy as jnp
from jax import lax
from jax.sharding import PartitionSpec as P

HD = 96


def probabilities(qh, kh):
    scores = jnp.dot(qh, kh.T, preferred_element_type=jnp.float32) * HD ** (-0.5)
    top = jnp.max(scores, axis=-1, keepdims=True)
    weights = jnp.exp(scores - top)
    return weights / jnp.sum(weights, axis=-1, keepdims=True)


def head_forward(qh, kh, vh):
    probs = probabilities(qh, kh).astype(jnp.bfloat16)
    return jnp.dot(probs, vh, preferred_element_type=jnp.float32).astype(jnp.bfloat16)


def head_backward(qh, kh, vh, dh):
    probs = probabilities(qh, kh)
    probs_b = probs.astype(jnp.bfloat16)
    dvalue = jnp.dot(probs_b.T, dh, preferred_element_type=jnp.float32).astype(jnp.bfloat16)
    dprobs = jnp.dot(dh, vh.T, preferred_element_type=jnp.float32)
    delta = jnp.sum(probs * dprobs, axis=-1, keepdims=True)
    dscore = (probs * (dprobs - delta) * HD ** (-0.5)).astype(jnp.bfloat16)
    dquery = jnp.dot(dscore, kh, preferred_element_type=jnp.float32).astype(jnp.bfloat16)
    dkey = jnp.dot(dscore.T, qh, preferred_element_type=jnp.float32).astype(jnp.bfloat16)
    return (dquery, dkey, dvalue)


def expert_core(rows_in, rows_grad, wgate, wup, wdown):
    gate = jnp.dot(rows_in, wgate, preferred_element_type=jnp.float32)
    upper = jnp.dot(rows_in, wup, preferred_element_type=jnp.float32)
    sig = jax.nn.sigmoid(gate)
    silu_gate = gate * sig
    act = (silu_gate * upper).astype(jnp.bfloat16)
    dact = lax.dot_general(
        rows_grad, wdown, (((1,), (1,)), ((), ())), preferred_element_type=jnp.float32
    )
    down_grad = lax.dot_general(
        act, rows_grad, (((0,), (0,)), ((), ())), preferred_element_type=jnp.float32
    )
    dsilu = sig * (1.0 + gate * (1.0 - sig))
    dgate = (dact * upper * dsilu).astype(jnp.bfloat16)
    dup = (dact * silu_gate).astype(jnp.bfloat16)
    return (dgate, dup, down_grad)


def slice_partial(dgate, dup, wgate, wup):
    joined = jnp.concatenate([dgate, dup], axis=1)
    weights = jnp.concatenate([wgate, wup], axis=1)
    return lax.dot_general(
        joined, weights, (((1,), (1,)), ((), ())), preferred_element_type=jnp.float32
    )


def split_heads(x):
    seqlen, cols = (x.shape[1], x.shape[2])
    return x[0].reshape(seqlen, cols // HD, HD).transpose(1, 0, 2)


def join_heads(x):
    count, seqlen, size = x.shape
    return x.transpose(1, 0, 2).reshape(1, seqlen, count * size)


def per_device(query, key_in, value, grad_out, expert_ids, gate_weights, w_gate, w_up, w_down):
    tokens = query.shape[1]
    width = query.shape[2]
    experts = lax.axis_size("seq")
    n_clips = lax.axis_size("dp")
    slots_per = 9 * tokens // (4 * experts)
    routed = 2 * tokens
    q_all, k_all, v_all = (
        lax.all_to_all(query, "seq", split_axis=2, concat_axis=1, tiled=True),
        lax.all_to_all(key_in, "seq", split_axis=2, concat_axis=1, tiled=True),
        lax.all_to_all(value, "seq", split_axis=2, concat_axis=1, tiled=True),
    )
    qh, kh, vh = (split_heads(q_all), split_heads(k_all), split_heads(v_all))
    heads_mixed = jax.vmap(head_forward)(qh, kh, vh)
    mixed = lax.all_to_all(join_heads(heads_mixed), "seq", split_axis=1, concat_axis=2, tiled=True)
    ids = expert_ids[0].reshape(routed)
    onehot = (ids[:, None] == jnp.arange(experts, dtype=jnp.int32)[None, :]).astype(jnp.int32)
    slots = jnp.sum((jnp.cumsum(onehot, axis=0) - onehot) * onehot, axis=1)
    place = (ids[None, None, :] == jnp.arange(experts, dtype=jnp.int32)[:, None, None]) & (
        slots[None, None, :] == jnp.arange(slots_per, dtype=jnp.int32)[None, :, None]
    )
    place = place.astype(jnp.bfloat16).reshape(experts * slots_per, routed)
    rows_mixed = jnp.repeat(mixed[0], 2, axis=0)
    scaled = (gate_weights[0][:, :, None] * grad_out[0].astype(jnp.float32)[:, None, :]).astype(
        jnp.bfloat16
    )
    scaled = scaled.reshape(routed, width)
    send_in = (
        jnp.dot(place, rows_mixed, preferred_element_type=jnp.float32)
        .astype(jnp.bfloat16)
        .reshape(experts, slots_per, width)
    )
    send_grad = (
        jnp.dot(place, scaled, preferred_element_type=jnp.float32)
        .astype(jnp.bfloat16)
        .reshape(experts, slots_per, width)
    )
    own_in, own_grad = (
        lax.all_to_all(send_in, "seq", split_axis=0, concat_axis=0, tiled=True),
        lax.all_to_all(send_grad, "seq", split_axis=0, concat_axis=0, tiled=True),
    )
    all_in, all_grad = (
        lax.all_gather(own_in, "dp", axis=0, tiled=True),
        lax.all_gather(own_grad, "dp", axis=0, tiled=True),
    )
    total_rows = n_clips * experts * slots_per
    dgate, dup, down_grad = expert_core(
        all_in.reshape(total_rows, width),
        all_grad.reshape(total_rows, width),
        w_gate[0],
        w_up[0],
        w_down[0],
    )
    partial_value = slice_partial(dgate, dup, w_gate[0], w_up[0]).reshape(
        n_clips * experts, slots_per, width
    )
    summed = lax.psum_scatter(
        partial_value.astype(jnp.bfloat16), "dp", scatter_dimension=0, tiled=True
    )
    back = lax.all_to_all(summed, "seq", split_axis=0, concat_axis=0, tiled=True)
    back_rows = jnp.dot(
        place.T, back.reshape(experts * slots_per, width), preferred_element_type=jnp.float32
    ).reshape(tokens, 2, width)
    dmixed = (grad_out[0].astype(jnp.float32) + back_rows[:, 0] + back_rows[:, 1]).astype(
        jnp.bfloat16
    )
    d_all = lax.all_to_all(dmixed[None], "seq", split_axis=2, concat_axis=1, tiled=True)
    dq, dk, dv = jax.vmap(head_backward)(qh, kh, vh, split_heads(d_all))
    grad_query, grad_key, grad_value = (
        lax.all_to_all(join_heads(dq), "seq", split_axis=1, concat_axis=2, tiled=True),
        lax.all_to_all(join_heads(dk), "seq", split_axis=1, concat_axis=2, tiled=True),
        lax.all_to_all(join_heads(dv), "seq", split_axis=1, concat_axis=2, tiled=True),
    )
    return (grad_query, grad_key, grad_value, down_grad.astype(jnp.bfloat16)[None])


def solution(mesh):
    return jax.shard_map(
        per_device,
        mesh=mesh,
        in_specs=(
            P("dp", "seq", None),
            P("dp", "seq", None),
            P("dp", "seq", None),
            P("dp", "seq", None),
            P("dp", "seq", None),
            P("dp", "seq", None),
            P("seq", None, "dp"),
            P("seq", None, "dp"),
            P("seq", "dp", None),
        ),
        out_specs=(
            P("dp", "seq", None),
            P("dp", "seq", None),
            P("dp", "seq", None),
            P("seq", "dp", None),
        ),
        check_vma=False,
    )
```

profile of v0, /device:TPU:10, one launch (start us, length us, event | category | flops | bytes accessed | tf_op | source)
XLA Modules:
  0.0 530.3 jit_solution(4105401418898868138)
XLA Ops:
  7.2 0.9 copy.73
  9.5 1.1 convert_bitcast_fusion
  12.3 1.3 convolution_convert_fusion.3
  13.6 1.4 reshape.236
  15.1 25.2 %all_to_all.144 = bf16[16,18,1536]{2,1,0:T(8,128)(2,1)S(1)} all-to-all(bf16[16,18,1536]{2,1,0:T(8,128)(2,1)S(1)} %reshape.236), channel_id=1, replica_groups=mesh['dp'=8,'seq'=16] {'seq'}, dimensions={0} | all-to-all | bytes 1769472 | tf_op jit(solution)/shard_map/all_to_all | solution.py:108
  40.3 1.2 copy.78
  42.6 8.8 %reduce.8 = bf16[1536,128]{1,0:T(8,128)(2,1)S(1)} reduce(bf16[1536,1,128]{2,1,0:T(2,128)(2,1)S(1)} %bitcast.194, bf16[]{:T(256)} %broadcast.114), dimensions={1}, to_apply=%bitcast.149.reduce_sub_computation | reduce | bytes 786434
  52.3 5.1 all-to-all-start.1
  57.4 2.2 copy.69
  59.5 8.8 %reduce.9 = bf16[1536,128]{1,0:T(8,128)(2,1)S(1)} reduce(bf16[1536,1,128]{2,1,0:T(2,128)(2,1)S(1)} %bitcast.200, bf16[]{:T(256)} %broadcast.114), dimensions={1}, to_apply=%bitcast.151.reduce_sub_computation | reduce | bytes 786434
  69.2 7.6 %all-to-all-start = ((bf16[16,2,6144]{2,1,0:T(2,128)(2,1)}), bf16[16,2,6144]{2,1,0:T(2,128)(2,1)S(1)}, u32[]{:S(2)}, u32[]{:S(2)}) async-start(bf16[16,2,6144]{2,1,0:T(2,128)(2,1)} %reshape.254), calls=%async_computation | async-start | bytes 786432 | tf_op jit(solution)/shard_map/all_to_all | solution.py:77
  76.8 2.2 copy.80
  79.0 8.8 %reduce.10 = bf16[1536,128]{1,0:T(8,128)(2,1)S(1)} reduce(bf16[1536,1,128]{2,1,0:T(2,128)(2,1)S(1)} %bitcast.201, bf16[]{:T(256)} %broadcast.114), dimensions={1}, to_apply=%bitcast.147.reduce_sub_computation | reduce | bytes 786434
  87.8 0.8 reshape.250
  88.7 7.2 %all-to-all-start.3 = ((bf16[16,2,6144]{2,1,0:T(2,128)(2,1)}), bf16[16,2,6144]{2,1,0:T(2,128)(2,1)S(1)}, u32[]{:S(2)}, u32[]{:S(2)}) async-start(bf16[16,2,6144]{2,1,0:T(2,128)(2,1)} %reshape.250), calls=%async_computation.3 | async-start | bytes 786432 | tf_op jit(solution)/shard_map/all_to_all | solution.py:79
  96.6 0.9 reshape_squeeze.6
  97.9 0.9 copy.70
  98.8 4.3 all-to-all-done.3
  103.7 9.2 %multiply_reduce_fusion.1 = (f32[2048]{0:T(1024)S(1)}, f32[2048,2048]{0,1:T(8,128)}) fusion(bf16[2048,1,96]{0,2,1:T(8,128)(2,1)} %reshape_squeeze.6, bf16[12,8,16,128]{3,2,1,0:T(8,128)(2,1)} %bitcast.219), kind=kOutput, calls=%fused_computation.3 | convolution fusion | flops 813692928 | bytes 17571840 | tf_op jit(solution)/shard_map/vmap()/dot_general | solution.py:10
  112.9 8.5 %fusion.1 = f32[2048]{0:T(1024)S(1)} fusion(f32[2048,2048]{0,1:T(8,128)} %get-tuple-element.19, f32[2048]{0:T(1024)S(1)} %get-tuple-element.18), kind=kLoop, calls=%fused_computation.5 | loop fusion | flops 12580864 | bytes 16793600 | tf_op jit(solution)/shard_map/vmap()/reduce_sum | solution.py:13
  121.5 7.7 %fusion.25 = bf16[1,2048,96]{1,2,0:T(8,128)(2,1)S(1)} fusion(bf16[12,8,16,128]{3,2,1,0:T(8,128)(2,1)S(1)} %bitcast.202, f32[2048,2048]{0,1:T(8,128)} %get-tuple-element.19, f32[2048]{0:T(1024)S(1)} %fusion.1, f32[2048]{0:T(1024)S(1)} %get-tuple-element.18), kind=kOutput, calls=%fused_computation.33 | convolution fusion | flops 822280192 | bytes 17580032 | tf_op jit(solution)/shard_map/vmap()/dot_general | solution.py:18
  129.9 21.0 %reduce.11 = bf16[2048,96]{1,0:T(8,128)(2,1)S(1)} reduce(bf16[2048,1,96]{2,1,0:T(2,128)(2,1)S(1)} %bitcast.187, bf16[]{:T(256)} %broadcast.114), dimensions={1}, to_apply=%bitcast.153.reduce_sub_computation | reduce | bytes 786434
  151.8 12.6 %all_to_all.145 = bf16[16,2,6144]{2,1,0:T(2,128)(2,1)S(1)} all-to-all(bf16[16,2,6144]{2,1,0:T(2,128)(2,1)S(1)} %reshape.256), channel_id=1, replica_groups=mesh['dp'=8,'seq'=16] {'seq'}, dimensions={0} | all-to-all | bytes 786432 | tf_op jit(solution)/shard_map/all_to_all | solution.py:83
  166.9 2.2 convolution_convert_fusion.2
  169.2 1.4 reshape.240
  170.6 17.4 %all_to_all.146 = bf16[16,18,1536]{2,1,0:T(8,128)(2,1)S(1)} all-to-all(bf16[16,18,1536]{2,1,0:T(8,128)(2,1)S(1)} %reshape.240), channel_id=1, replica_groups=mesh['dp'=8,'seq'=16] {'seq'}, dimensions={0} | all-to-all | bytes 1769472 | tf_op jit(solution)/shard_map/all_to_all | solution.py:107
  188.0 1.2 copy.86
  189.3 11.3 %copy.79 = bf16[128,18,1536]{2,1,0:T(8,128)(2,1)} copy(bf16[128,18,1536]{2,0,1:T(8,128)(2,1)} %all-gather.3.cloned.1.call-done) | data formatting | bytes 14155776 | tf_op jit(solution)/shard_map/all_gather | solution.py:112
  200.6 11.2 %reshape.237 = bf16[2304,1536]{1,0:T(8,128)(2,1)} reshape(bf16[128,18,1536]{2,1,0:T(8,128)(2,1)} %copy.79) | data formatting | bytes 14155776 | tf_op jit(solution)/shard_map/reshape | solution.py:117
  211.9 8.6 %fusion.28 = f32[2304,512]{0,1:T(8,128)} fusion(bf16[2304,1536]{1,0:T(8,128)(2,1)} %reshape.237, bf16[1,512,1536]{2,1,0:T(8,128)(2,1)S(1)} %copy-done), kind=kOutput, calls=%fused_computation.34 | convolution fusion | flops 3623878656 | bytes 13369344 | tf_op jit(solution)/shard_map/dot_general | solution.py:39
  220.4 11.3 %all-gather.5.cloned.1.call-done = bf16[128,18,1536]{2,0,1:T(8,128)(2,1)} async-done(((bf16[16,18,1536]{2,0,1:T(8,128)(2,1)}), bf16[128,18,1536]{2,0,1:T(8,128)(2,1)}) %all-gather.5.cloned.1.call-update) | async-done | bytes 7077904 | tf_op jit(solution)/shard_map/all_gather | solution.py:111
  231.7 10.7 %copy.87 = bf16[128,18,1536]{2,1,0:T(8,128)(2,1)} copy(bf16[128,18,1536]{2,0,1:T(8,128)(2,1)} %all-gather.5.cloned.1.call-done) | data formatting | bytes 14155776 | tf_op jit(solution)/shard_map/all_gather | solution.py:111
  242.4 11.4 %reshape.241 = bf16[2304,1536]{1,0:T(8,128)(2,1)} reshape(bf16[128,18,1536]{2,1,0:T(8,128)(2,1)} %copy.87) | data formatting | bytes 14155776 | tf_op jit(solution)/shard_map/reshape | solution.py:116
  253.8 8.7 %fusion.58 = f32[2304,512]{0,1:T(8,128)} fusion(bf16[2304,1536]{1,0:T(8,128)(2,1)} %reshape.241, bf16[1,1536,512]{2,1,0:T(8,128)(2,1)S(1)} %copy-done.11), kind=kOutput, calls=%fused_computation.76 | convolution fusion | flops 3623878656 | bytes 13369344 | tf_op jit(solution)/shard_map/dot_general | solution.py:35
  262.6 10.5 %multiply_convert_fusion.3 = (bf16[2304,512]{0,1:T(8,128)(2,1)}, bf16[2304,512]{0,1:T(8,128)(2,1)}, f32[2304,512]{0,1:T(8,128)}) fusion(f32[2304,512]{0,1:T(8,128)} %fusion.28, f32[2304,512]{0,1:T(8,128)} %fusion.58, bf16[2304,1536]{1,0:T(8,128)(2,1)S(1)} %copy-done.3, bf16[1,1536,512]{2,1,0:T(8,128)(2,1)S(1)} %copy-done.12), kind=kOutput, calls=%fused_computation.12 | convolution fusion | flops 3639214080 | bytes 27525120 | tf_op jit(solution)/shard_map/dot_general | solution.py:34
  273.1 12.3 %convolution_convert_fusion = bf16[2304,1536]{1,0:T(8,128)(2,1)} fusion(bf16[2304,512]{0,1:T(8,128)(2,1)} %get-tuple-element.17, bf16[2304,512]{0,1:T(8,128)(2,1)} %get-tuple-element.16, bf16[1536,512]{1,0:T(8,128)(2,1)S(1)} %bitcast.225, bf16[1536,512]{1,0:T(8,128)(2,1)S(1)} %bitcast.226), kind=kOutput, calls=%fused_computation.6 | convolution fusion | flops 7267024896 | bytes 14942208 | tf_op jit(solution)/shard_map/dot_general | solution.py:54
  285.4 11.0 %convert_element_type.111 = bf16[128,18,1536]{2,1,0:T(8,128)(2,1)} reshape(bf16[2304,1536]{1,0:T(8,128)(2,1)} %convolution_convert_fusion) | data formatting | bytes 14155776 | tf_op jit(solution)/shard_map/convert_element_type | solution.py:126
  296.4 56.4 %reduce-scatter.2.cloned.1.call-done = bf16[16,18,1536]{2,1,0:T(8,128)(2,1)} async-done(((bf16[128,18,1536]{2,1,0:T(8,128)(2,1)}), bf16[16,18,1536]{2,1,0:T(8,128)(2,1)}) %reduce-scatter.2.cloned.1.call-update) | async-done | bytes 884752 | tf_op jit(solution)/shard_map/reduce_scatter | solution.py:125
  352.7 7.4 %all-to-all-start.6 = ((bf16[16,18,1536]{2,1,0:T(8,128)(2,1)}), bf16[16,18,1536]{2,1,0:T(8,128)(2,1)S(1)}, u32[]{:S(2)}, u32[]{:S(2)}) async-start(bf16[16,18,1536]{2,1,0:T(8,128)(2,1)} %reduce-scatter.2.cloned.1.call-done), calls=%async_computation.7 | async-start | bytes 2359296 | tf_op jit(solution)/shard_map/all_to_all | solution.py:128
  360.5 18.0 %all-to-all-done.6 = bf16[16,18,1536]{2,1,0:T(8,128)(2,1)S(1)} async-done(((bf16[16,18,1536]{2,1,0:T(8,128)(2,1)}), bf16[16,18,1536]{2,1,0:T(8,128)(2,1)S(1)}, u32[]{:S(2)}, u32[]{:S(2)}) %all-to-all-start.6) | async-done | bytes 884768 | tf_op jit(solution)/shard_map/all_to_all | solution.py:128
  380.0 8.8 %reduce.12 = bf16[1536,128]{1,0:T(8,128)(2,1)S(1)} reduce(bf16[1536,1,128]{2,1,0:T(2,128)(2,1)S(1)} %bitcast.198, bf16[]{:T(256)} %broadcast.114), dimensions={1}, to_apply=%bitcast.155.reduce_sub_computation | reduce | bytes 786434
  388.9 0.8 reshape.258
  389.7 6.8 %all-to-all-start.7 = ((bf16[16,2,6144]{2,1,0:T(2,128)(2,1)}), bf16[16,2,6144]{2,1,0:T(2,128)(2,1)S(1)}, u32[]{:S(2)}, u32[]{:S(2)}) async-start(bf16[16,2,6144]{2,1,0:T(2,128)(2,1)} %reshape.258), calls=%async_computation.8 | async-start | bytes 786432 | tf_op jit(solution)/shard_map/all_to_all | solution.py:135
  396.7 7.8 %all-to-all-done.7 = bf16[16,2,6144]{2,1,0:T(2,128)(2,1)S(1)} async-done(((bf16[16,2,6144]{2,1,0:T(2,128)(2,1)}), bf16[16,2,6144]{2,1,0:T(2,128)(2,1)S(1)}, u32[]{:S(2)}, u32[]{:S(2)}) %all-to-all-start.7) | async-done | bytes 393248 | tf_op jit(solution)/shard_map/all_to_all | solution.py:135
  405.1 7.7 %fusion.22 = bf16[1,2048,96]{1,2,0:T(8,128)(2,1)S(1)} fusion(bf16[12,8,16,128]{3,2,1,0:T(8,128)(2,1)S(1)} %bitcast.222, f32[2048,2048]{0,1:T(8,128)} %get-tuple-element.19, f32[2048]{0:T(1024)S(1)} %fusion.1, f32[2048]{0:T(1024)S(1)} %get-tuple-element.18), kind=kOutput, calls=%fused_computation.32 | convolution fusion | flops 822280192 | bytes 17580032 | tf_op jit(solution)/shard_map/vmap()/dot_general | solution.py:24
  413.6 11.6 %reduce.15 = bf16[2048,96]{1,0:T(8,128)(2,1)S(1)} reduce(bf16[2048,1,96]{2,1,0:T(2,128)(2,1)S(1)} %bitcast.189, bf16[]{:T(256)} %broadcast.114), dimensions={1}, to_apply=%bitcast.161.reduce_sub_computation | reduce | bytes 786434
  425.2 1.6 reshape.264
  426.8 5.9 %all-to-all-start.10 = ((bf16[16,2,6144]{2,1,0:T(2,128)(2,1)}), bf16[16,2,6144]{2,1,0:T(2,128)(2,1)S(1)}, u32[]{:S(2)}, u32[]{:S(2)}) async-start(bf16[16,2,6144]{2,1,0:T(2,128)(2,1)} %reshape.264), calls=%async_computation.11 | async-start | bytes 786432 | tf_op jit(solution)/shard_map/all_to_all | solution.py:140
  432.7 8.2 %multiply_reduce_fusion = (f32[2048]{0:T(1024)S(1)}, f32[2048,2048]{0,1:T(8,128)S(1)}) fusion(f32[2048]{0:T(1024)S(1)} %fusion.1, f32[2048]{0:T(1024)S(1)} %get-tuple-element.18, f32[2048,2048]{0,1:T(8,128)} %get-tuple-element.19, bf16[2048,1,96]{0,2,1:T(8,128)(2,1)S(1)} %reshape_squeeze.7, bf16[12,8,16,128]{3,2,1,0:T(8,128)(2,1)S(1)} %bitcast.223), kind=kOutput, calls=%fused_computation.1 | convolution fusion | flops 826275840 | bytes 34365440 | tf_op jit(solution)/shard_map/vmap()/dot_general | solution.py:25
  440.9 8.5 %multiply_convert_fusion = bf16[2048,2048]{0,1:T(8,128)(2,1)S(1)} fusion(f32[2048,2048]{0,1:T(8,128)S(1)} %get-tuple-element.22, f32[2048]{0:T(1024)S(1)} %get-tuple-element.21, f32[2048]{0:T(1024)S(1)} %fusion.1, f32[2048]{0:T(1024)S(1)} %get-tuple-element.18, f32[2048,2048]{0,1:T(8,128)} %get-tuple-element.19), kind=kLoop, calls=%fused_computation | loop fusion | flops 29360128 | bytes 41967616 | tf_op jit(solution)/shard_map/vmap()/convert_element_type | solution.py:27
  449.4 3.2 copy-done.2
  452.6 2.7 fusion.20
  456.1 11.6 %reduce.14 = bf16[2048,96]{1,0:T(8,128)(2,1)S(1)} reduce(bf16[2048,1,96]{2,1,0:T(2,128)(2,1)S(1)} %bitcast.190, bf16[]{:T(256)} %broadcast.114), dimensions={1}, to_apply=%bitcast.159.reduce_sub_computation | reduce | bytes 786434
  467.6 1.6 reshape.262
  469.2 7.6 %all-to-all-start.9 = ((bf16[16,2,6144]{2,1,0:T(2,128)(2,1)}), bf16[16,2,6144]{2,1,0:T(2,128)(2,1)S(1)}, u32[]{:S(2)}, u32[]{:S(2)}) async-start(bf16[16,2,6144]{2,1,0:T(2,128)(2,1)} %reshape.262), calls=%async_computation.10 | async-start | bytes 786432 | tf_op jit(solution)/shard_map/all_to_all | solution.py:139
  476.8 4.8 fusion.21
  482.4 11.6 %reduce.13 = bf16[2048,96]{1,0:T(8,128)(2,1)S(1)} reduce(bf16[2048,1,96]{2,1,0:T(2,128)(2,1)S(1)} %bitcast.186, bf16[]{:T(256)} %broadcast.114), dimensions={1}, to_apply=%bitcast.157.reduce_sub_computation | reduce | bytes 786434
  494.0 1.6 reshape.260
  495.6 7.7 %all-to-all-start.8 = ((bf16[16,2,6144]{2,1,0:T(2,128)(2,1)}), bf16[16,2,6144]{2,1,0:T(2,128)(2,1)}, u32[]{:S(2)}, u32[]{:S(2)}) async-start(bf16[16,2,6144]{2,1,0:T(2,128)(2,1)} %reshape.260), calls=%async_computation.9 | async-start | bytes 786432 | tf_op jit(solution)/shard_map/all_to_all | solution.py:138
  503.2 10.8 %fusion.13 = bf16[1,512,1536]{2,1,0:T(8,128)(2,1)} fusion(bf16[2304,1536]{1,0:T(8,128)(2,1)} %reshape.237, f32[2304,512]{0,1:T(8,128)} %fusion.58, f32[2304,512]{0,1:T(8,128)} %get-tuple-element.20), kind=kOutput, calls=%fused_computation.23 | convolution fusion | flops 3631742976 | bytes 18087936 | tf_op jit(solution)/shard_map/dot_general | solution.py:42
  515.7 0.9 copy.104
  518.2 0.9 copy.103
  519.1 2.4 reshape.261
  522.3 0.9 copy.102
  (97 shorter events, 20.6 us)
Async XLA Ops:
  7.2 204.7 %copy-start = (bf16[1,512,1536]{2,1,0:T(8,128)(2,1)S(1)}, bf16[1,512,1536]{2,1,0:T(8,128)(2,1)}, u32[]{:S(2)}) copy-start(bf16[1,512,1536]{2,1,0:T(8,128)(2,1)} %param.17) | copy-start | bytes 4718596
  7.2 182.1 %all-gather.3.cloned.1.call-start = ((), (), s32[]{:S(2)}) async-start(), calls=%async_computation.12 | async-start | bytes 7962624 | tf_op jit(solution)/shard_map/all_gather | solution.py:112
  9.5 32.6 %copy-start.8 = (pred[288,256]{1,0:T(32,128)(4,1)}, pred[288,256]{1,0:T(32,128)(4,1)S(1)}, u32[]{:S(2)}) copy-start(pred[288,256]{1,0:T(32,128)(4,1)S(1)} %and.31) | copy-start | bytes 221188
  13.6 27.8 %copy-start.10 = (bf16[1,128,1536]{2,1,0:T(8,128)(2,1)S(1)}, bf16[1,128,1536]{2,1,0:T(8,128)(2,1)}, u32[]{:S(2)}) copy-start(bf16[1,128,1536]{2,1,0:T(8,128)(2,1)} %param.10) | copy-start | bytes 1179652
  52.3 16.9 %all-to-all-start.1 = ((bf16[16,2,6144]{2,1,0:T(2,128)(2,1)}), bf16[16,2,6144]{2,1,0:T(2,128)(2,1)S(1)}, u32[]{:S(2)}, u32[]{:S(2)}) async-start(bf16[16,2,6144]{2,1,0:T(2,128)(2,1)} %reshape.252), calls=%async_computation.1 | async-start | bytes 786432 | tf_op jit(solution)/shard_map/all_to_all | solution.py:78
  69.2 19.4 %all-to-all-start = ((bf16[16,2,6144]{2,1,0:T(2,128)(2,1)}), bf16[16,2,6144]{2,1,0:T(2,128)(2,1)S(1)}, u32[]{:S(2)}, u32[]{:S(2)}) async-start(bf16[16,2,6144]{2,1,0:T(2,128)(2,1)} %reshape.254), calls=%async_computation | async-start | bytes 786432 | tf_op jit(solution)/shard_map/all_to_all | solution.py:77
  88.7 14.4 %all-to-all-start.3 = ((bf16[16,2,6144]{2,1,0:T(2,128)(2,1)}), bf16[16,2,6144]{2,1,0:T(2,128)(2,1)S(1)}, u32[]{:S(2)}, u32[]{:S(2)}) async-start(bf16[16,2,6144]{2,1,0:T(2,128)(2,1)} %reshape.250), calls=%async_computation.3 | async-start | bytes 786432 | tf_op jit(solution)/shard_map/all_to_all | solution.py:79
  95.9 135.8 %all-gather.5.cloned.1.call-start = ((), (), s32[]{:S(2)}) async-start(), calls=%async_computation.13 | async-start | bytes 7962624 | tf_op jit(solution)/shard_map/all_gather | solution.py:111
  96.5 16.4 %copy-start.4 = (bf16[1,16,128,96]{2,1,3,0:T(8,128)(2,1)}, bf16[1,16,128,96]{2,1,3,0:T(8,128)(2,1)S(1)}, u32[]{:S(2)}) copy-start(bf16[1,16,128,96]{2,1,3,0:T(8,128)(2,1)S(1)} %copy.72) | copy-start | bytes 1179652
  189.2 163.5 %reduce-scatter.2.cloned.1.call-start = ((), (), s32[]{:S(2)}) async-start(), calls=%async_computation.14 | async-start | bytes 10616832 | tf_op jit(solution)/shard_map/reduce_scatter | solution.py:125
  242.4 11.4 %copy-start.11 = (bf16[1,1536,512]{2,1,0:T(8,128)(2,1)S(1)}, bf16[1,1536,512]{2,1,0:T(8,128)(2,1)}, u32[]{:S(2)}) copy-start(bf16[1,1536,512]{2,1,0:T(8,128)(2,1)} %param.16) | copy-start | bytes 4718596
  253.8 8.7 %copy-start.3 = (bf16[2304,1536]{1,0:T(8,128)(2,1)S(1)}, bf16[2304,1536]{1,0:T(8,128)(2,1)}, u32[]{:S(2)}) copy-start(bf16[2304,1536]{1,0:T(8,128)(2,1)} %reshape.241) | copy-start | bytes 21233668
  253.8 8.7 %copy-start.12 = (bf16[1,1536,512]{2,1,0:T(8,128)(2,1)S(1)}, bf16[1,1536,512]{2,1,0:T(8,128)(2,1)}, u32[]{:S(2)}) copy-start(bf16[1,1536,512]{2,1,0:T(8,128)(2,1)} %param.15) | copy-start | bytes 4718596
  296.4 63.8 %copy-start.9 = (pred[288,256]{1,0:T(32,128)(4,1)S(1)}, pred[288,256]{1,0:T(32,128)(4,1)}, u32[]{:S(2)}) copy-start(pred[288,256]{1,0:T(32,128)(4,1)} %copy-done.8) | copy-start | bytes 221188
  296.4 83.0 %copy-start.6 = (bf16[1,128,1536]{2,1,0:T(8,128)(2,1)S(1)}, bf16[1,128,1536]{2,1,0:T(8,128)(2,1)}, u32[]{:S(2)}) copy-start(bf16[1,128,1536]{2,1,0:T(8,128)(2,1)} %param.12) | copy-start | bytes 1179652
  352.7 25.7 %all-to-all-start.6 = ((bf16[16,18,1536]{2,1,0:T(8,128)(2,1)}), bf16[16,18,1536]{2,1,0:T(8,128)(2,1)S(1)}, u32[]{:S(2)}, u32[]{:S(2)}) async-start(bf16[16,18,1536]{2,1,0:T(8,128)(2,1)} %reduce-scatter.2.cloned.1.call-done), calls=%async_computation.7 | async-start | bytes 2359296 | tf_op jit(solution)/shard_map/all_to_all | solution.py:128
  389.7 14.8 %all-to-all-start.7 = ((bf16[16,2,6144]{2,1,0:T(2,128)(2,1)}), bf16[16,2,6144]{2,1,0:T(2,128)(2,1)S(1)}, u32[]{:S(2)}, u32[]{:S(2)}) async-start(bf16[16,2,6144]{2,1,0:T(2,128)(2,1)} %reshape.258), calls=%async_computation.8 | async-start | bytes 786432 | tf_op jit(solution)/shard_map/all_to_all | solution.py:135
  426.8 42.5 %all-to-all-start.10 = ((bf16[16,2,6144]{2,1,0:T(2,128)(2,1)}), bf16[16,2,6144]{2,1,0:T(2,128)(2,1)S(1)}, u32[]{:S(2)}, u32[]{:S(2)}) async-start(bf16[16,2,6144]{2,1,0:T(2,128)(2,1)} %reshape.264), calls=%async_computation.11 | async-start | bytes 786432 | tf_op jit(solution)/shard_map/all_to_all | solution.py:140
  440.9 11.7 %copy-start.7 = (bf16[1,16,128,96]{2,1,3,0:T(8,128)(2,1)S(1)}, bf16[1,16,128,96]{2,1,3,0:T(8,128)(2,1)}, u32[]{:S(2)}) copy-start(bf16[1,16,128,96]{2,1,3,0:T(8,128)(2,1)} %copy.70) | copy-start | bytes 1179652
  449.4 3.2 copy-start.2
  452.6 24.2 %copy-start.5 = (bf16[1,16,128,96]{2,1,3,0:T(8,128)(2,1)S(1)}, bf16[1,16,128,96]{2,1,3,0:T(8,128)(2,1)}, u32[]{:S(2)}) copy-start(bf16[1,16,128,96]{2,1,3,0:T(8,128)(2,1)} %copy-done.4) | copy-start | bytes 1179652
  469.2 26.3 %all-to-all-start.9 = ((bf16[16,2,6144]{2,1,0:T(2,128)(2,1)}), bf16[16,2,6144]{2,1,0:T(2,128)(2,1)S(1)}, u32[]{:S(2)}, u32[]{:S(2)}) async-start(bf16[16,2,6144]{2,1,0:T(2,128)(2,1)} %reshape.262), calls=%async_computation.10 | async-start | bytes 786432 | tf_op jit(solution)/shard_map/all_to_all | solution.py:139
  495.6 23.6 %all-to-all-start.8 = ((bf16[16,2,6144]{2,1,0:T(2,128)(2,1)}), bf16[16,2,6144]{2,1,0:T(2,128)(2,1)}, u32[]{:S(2)}, u32[]{:S(2)}) async-start(bf16[16,2,6144]{2,1,0:T(2,128)(2,1)} %reshape.260), calls=%async_computation.9 | async-start | bytes 786432 | tf_op jit(solution)/shard_map/all_to_all | solution.py:138
  514.8 8.4 %copy-start.1 = (bf16[1,512,1536]{2,1,0:T(8,128)(2,1)S(1)}, bf16[1,512,1536]{2,1,0:T(8,128)(2,1)}, u32[]{:S(2)}) copy-start(bf16[1,512,1536]{2,1,0:T(8,128)(2,1)} %param.17) | copy-start | bytes 4718596
Sparse Core Ops, SparseCore 0:
  41.6 42.3 all-gather.2
  189.4 42.2 all-gather.4
  296.5 56.1 reduce-scatter.1
where the time goes:
time: 540 us; the launch traced here: 530 us
  other arithmetic  111 us (21%)
  local copies, waits for them, and re-layouts  101 us (19%)
  waiting for transfers between devices  97.8 us (18%)
  matrix products  95.4 us (18%)
  starting transfers between devices  55.3 us (10%)
  blocking collectives  55.3 us (10%)
  between operations  14.9 us (3%)
    unnamed x8, other arithmetic  91.1 us
    reduce_scatter x1, waiting for transfers between devices, per_device(): lax.psum_scatter(partial_value.astype(jnp.bfloat16), 'dp', scatter_dimens...  56.4 us
    unnamed x58, local copies, waits for them, and re-layouts  28.1 us
    all_to_all x1, blocking collectives, per_device(): lax.all_to_all(send_grad, 'seq', split_axis=0, concat_axis=0, tiled=True)  25.2 us
    all_to_all x1, waiting for transfers between devices, per_device(): lax.all_to_all(summed, 'seq', split_axis=0, concat_axis=0, tiled=True)  18 us
    all_to_all x1, blocking collectives, per_device(): lax.all_to_all(send_in, 'seq', split_axis=0, concat_axis=0, tiled=True)  17.4 us
    all_to_all x1, blocking collectives, per_device(): lax.all_to_all(join_heads(heads_mixed), 'seq', split_axis=1, concat_axis=...  12.6 us
    dot_general x1, matrix products, slice_partial(): lax.dot_general(joined, weights, (((1,), (1,)), ((), ())), preferred_elem...  12.3 us
  transfers between devices with their start and end apart: 11, of which 5 were waited for; matrix products, arithmetic and copies ran while one was open for 36% of the time, Pallas kernels for 0%

commit v1 on v0

v1 whole, which is shorter than its diff:
```python
import jax
import jax.numpy as jnp
from jax import lax
from jax.experimental import pallas as pl
from jax.experimental.pallas import tpu as pltpu
from jax.sharding import PartitionSpec as P

bf = jnp.bfloat16
f32 = jnp.float32
MESH = pl.DeviceIdType.MESH
HD = 96
SC = HD ** -0.5
C2 = SC * 1.4426950408889634
VLIM = 62 << 20
ORDER = [1, 4, 3, 12, 5, 15, 7, 13, 8, 2, 9, 6, 11, 14, 10]


def nt(a, b):
    return lax.dot_general(a, b, (((1,), (1,)), ((), ())), preferred_element_type=f32)


def nn(a, b):
    return lax.dot_general(a, b, (((1,), (0,)), ((), ())), preferred_element_type=f32)


def tn(a, b):
    return lax.dot_general(a, b, (((0,), (0,)), ((), ())), preferred_element_type=f32)


def iota(shape, dim):
    return lax.broadcasted_iota(jnp.int32, shape, dim)


def onehot(cond):
    return jnp.where(cond, 1.0, 0.0).astype(bf)


class Place:
    def __init__(self):
        self.dp = lax.axis_index("dp")
        self.s = lax.axis_index("seq")
        self.x = self.s // 4
        self.z = lax.rem(self.s, 4)
        self.y = self.dp // 2
        self.core = lax.rem(self.dp, 2)

    def to(self, o):
        dx, dz = o // 4, lax.rem(o, 4) if not isinstance(o, int) else o % 4
        return lax.rem(self.x + dx, 4) * 4 + lax.rem(self.z + dz, 4)

    def source(self, o):
        dx, dz = o // 4, lax.rem(o, 4) if not isinstance(o, int) else o % 4
        return lax.rem(self.x + 4 - dx, 4) * 4 + lax.rem(self.z + 4 - dz, 4)

    def clip(self, k):
        return lax.rem(self.y + k, 4) * 2 + self.core

    def pair(self, k):
        return lax.rem(self.y + k, 4) * 2 + 1 - self.core


def greet(devices):
    b = pltpu.get_barrier_semaphore()
    for d in devices:
        pl.semaphore_signal(b, inc=1, device_id=d, device_id_type=MESH)


def greeted(n):
    pl.semaphore_wait(pltpu.get_barrier_semaphore(), n)


def rcopy(src, dst, ss, rs, dev):
    return pltpu.make_async_remote_copy(
        src_ref=src, dst_ref=dst, send_sem=ss, recv_sem=rs, device_id=dev, device_id_type=MESH
    )


class Exchange:
    def __init__(self, at, send, recv, ss, rs):
        self.at, self.send, self.recv, self.ss, self.rs = at, send, recv, ss, rs

    def out(self, o):
        t = self.at.to(o)
        return rcopy(self.send(t), self.recv(self.at.s), self.ss.at[o], self.rs.at[o], (self.at.dp, t))

    def into(self, o):
        t = self.at.source(o)
        return rcopy(self.send(t), self.recv(t), self.ss.at[o], self.rs.at[o], (self.at.dp, t))

    def start(self):
        for o in ORDER:
            self.out(o).start()

    def wait_recv(self):
        @pl.loop(1, 16)
        def _(o):
            self.into(o).wait_recv()

    def wait_send(self):
        @pl.loop(1, 16)
        def _(o):
            self.out(o).wait_send()


def seq_peers(at):
    return [(at.dp, at.to(o)) for o in ORDER]


def dp_peers(at):
    return [(at.clip(1), at.s), (at.clip(3), at.s), (at.clip(2), at.s), (at.pair(0), at.s)]


def main_places(M, b):
    io = iota((256, 128), 0).astype(f32)
    return onehot((io == M[b, 0:1, :]) | (io == M[b, 1:2, :]))


def extra_places(M, b):
    io = iota((512, 128), 0)
    low = lax.rem(io, 32)
    own = (low // 2) == b
    tgt = ((io // 32) * 2 + lax.rem(io, 2)).astype(f32)
    return onehot(own & ((tgt == M[b, 2:3, :]) | (tgt == M[b, 3:4, :])))


class Gather:
    def __init__(self, at, buf, ss, rs):
        self.at, self.buf, self.ss, self.rs = at, buf, ss, rs

    def half(self, c, i):
        return self.buf.at[c, pl.ds(144 * i, 144), :]

    def copy(self, n, c, i, dev):
        ref = self.half(c, i)
        return rcopy(ref, ref, self.ss.at[n], self.rs.at[n], (dev, self.at.s))

    def own_out(self):
        a = self.at
        for i in (0, 1):
            self.copy(i, a.clip(0), i, a.clip(1)).start()
            self.copy(2 + 1 - i, a.clip(0), 1 - i, a.clip(3)).start()
        for i in (0, 1):
            self.copy(6 + i, a.clip(0), i, a.pair(0)).start()

    def relay(self):
        a = self.at
        self.copy(0, a.clip(3), 0, a.clip(1)).wait_recv()
        self.copy(4, a.clip(3), 0, a.clip(1)).start()
        self.copy(8, a.clip(3), 0, a.pair(0)).start()
        self.copy(3, a.clip(1), 1, a.clip(3)).wait_recv()
        self.copy(5, a.clip(1), 1, a.clip(3)).start()
        self.copy(11, a.clip(1), 1, a.pair(0)).start()

    def rest(self):
        a = self.at
        self.copy(1, a.clip(3), 1, a.clip(1)).wait_recv()
        self.copy(9, a.clip(3), 1, a.pair(0)).start()
        self.copy(2, a.clip(1), 0, a.clip(3)).wait_recv()
        self.copy(10, a.clip(1), 0, a.pair(0)).start()

    def far(self):
        a = self.at
        self.copy(4, a.clip(2), 0, a.clip(1)).wait_recv()
        self.copy(12, a.clip(2), 0, a.pair(0)).start()
        self.copy(5, a.clip(2), 1, a.clip(3)).wait_recv()
        self.copy(13, a.clip(2), 1, a.pair(0)).start()

    def other(self, k):
        n = {0: 6, 3: 8, 1: 10, 2: 12}[k]
        for i in (0, 1):
            self.copy(n + i, self.at.pair(k), i, self.at.pair(0)).wait_recv()

    def wait_send(self):
        for n in range(14):
            self.copy(n, self.at.clip(0), 0, self.at.clip(1)).wait_send()


def attention(j, Q, K, Vt, ET, Oa, mixed, s_ref):
    CH = 512
    q0 = pl.multiple_of(j * 256, 256)
    Qj = Q[pl.ds(q0, 256), :]
    m = None
    for c in range(2048 // CH):
        s = nt(K[c * CH:(c + 1) * CH, :], Qj)
        s_ref[c * CH:(c + 1) * CH, :] = s
        mc = jnp.max(s.reshape(CH // 8, 8, 256), axis=0)
        m = mc if m is None else jnp.maximum(m, mc)
    m = jnp.max(m, axis=0, keepdims=True) * C2
    for c in range(2048 // CH):
        e = jnp.exp2(s_ref[c * CH:(c + 1) * CH, :] * C2 - m).astype(bf)
        ET[c * CH:(c + 1) * CH, pl.ds(q0, 256)] = e
    ot = nn(Vt[...], ET[:, pl.ds(q0, 256)])
    linv = 1.0 / ot[96:97, :]
    on = jnp.concatenate([ot[:96, :] * linv, jnp.broadcast_to(linv, (32, 256))], axis=0)
    o = on.T
    Oa[pl.ds(q0, 256), :] = o
    mixed[pl.ds(q0, 256), :] = o.astype(bf)


def front(q, k, v, go, meta, Q, K, V, G, ET, Oa, M, rows, SA,
          Sx, Rx, Ms, SM, RM, SX, RX, B, RB, Vt, mixed, s_ref,
          ss_x, rs_x, ss_m, rs_m, ss_s, rs_s, ss_e, rs_e, ss_b, rs_b, ss_g, rs_g):
    at = Place()
    greet(seq_peers(at) + dp_peers(at))

    e0, e1, g0, g1 = (meta[i:i + 1, :] for i in range(4))
    ie = iota((16, 128), 0).astype(f32)
    oh0, oh1 = jnp.where(ie == e0, 1.0, 0.0), jnp.where(ie == e1, 1.0, 0.0)
    before = onehot(iota((128, 128), 0) < iota((128, 128), 1))
    count = nn((oh0 + oh1).astype(bf), before)
    s0 = jnp.sum(oh0 * count, axis=0, keepdims=True)
    s1 = jnp.sum(oh1 * count, axis=0, keepdims=True)
    m0 = jnp.where(s0 < 16, e0 * 16 + s0, -1.0)
    m1 = jnp.where(s1 < 16, e1 * 16 + s1, -1.0)
    x0 = jnp.where(s0 < 16, -1.0, e0 * 2 + s0 - 16)
    x1 = jnp.where(s1 < 16, -1.0, e1 * 2 + s1 - 16)
    Ms[...] = jnp.concatenate([m0, m1, x0, x1, m0, m0, m0, m0], axis=0)

    io = iota((256, 128), 0).astype(f32)
    c0, c1 = io == m0, io == m1
    gw = jnp.sum(jnp.where(c0, g0, 0.0) + jnp.where(c1, g1, 0.0), axis=1, keepdims=True)
    pm = onehot(c0 | c1)
    for n in range(3):
        cols = slice(512 * n, 512 * n + 512)
        SM[:, :, cols] = (nn(pm, go[:, cols]) * gw).astype(bf).reshape(16, 16, 512)
    io = iota((32, 128), 0).astype(f32)
    c0, c1 = io == x0, io == x1
    gw = jnp.sum(jnp.where(c0, g0, 0.0) + jnp.where(c1, g1, 0.0), axis=1, keepdims=True)
    ext = (nn(onehot(c0 | c1), go[...]) * gw).astype(bf)
    stack = jnp.concatenate([ext[:, 128 * g:128 * g + 128] for g in range(12)], axis=0)
    r, c = iota((512, 384), 0), iota((512, 384), 1)
    low = lax.rem(r, 32)
    spread = onehot(c == (low // 2) * 32 + (r // 32) * 2 + lax.rem(low, 2))
    SX[...] = nn(spread, stack).astype(bf).reshape(16, 32, 128)

    for n, ref in enumerate((q, k, v, go)):
        for h in range(16):
            Sx[n, h] = jnp.concatenate(
                [ref[32 * g:32 * g + 32, 96 * h:96 * h + 96] for g in range(4)], axis=1)

    greeted(19)
    xm = Exchange(at, lambda t: Ms, lambda t: M.at[t], ss_m, rs_m)
    xs = Exchange(at, lambda t: SM.at[t], lambda t: RM.at[t], ss_s, rs_s)
    xe = Exchange(at, lambda t: SX.at[t], lambda t: RX.at[t], ss_e, rs_e)
    xq = [Exchange(at, lambda t, n=n: Sx.at[n, t], lambda t, n=n: Rx.at[n, t], ss_x.at[n], rs_x.at[n])
          for n in range(4)]
    xs.start()
    xe.start()
    for n in range(4):
        xq[n].start()
    xm.start()
    M[at.s] = Ms[...]
    RM[at.s] = SM[at.s]
    RX[at.s] = SX[at.s]
    for n in range(4):
        Rx[n, at.s] = Sx[n, at.s]

    xs.wait_recv()
    SA[at.dp, 0:256, :] = RM[...].reshape(256, 1536)
    xe.wait_recv()
    r, c = iota((384, 512), 1), iota((384, 512), 0)
    low = lax.rem(r, 32)
    pick = onehot(c == (low // 2) * 32 + (r // 32) * 2 + lax.rem(low, 2))
    back = nn(pick, RX[...].reshape(512, 128)).astype(bf)
    SA[at.dp, 256:288, :] = jnp.concatenate([back[32 * g:32 * g + 32] for g in range(12)], axis=1)
    ga = Gather(at, SA, ss_g, rs_g)
    ga.own_out()

    def unpack(n, dst, fill):
        @pl.loop(0, 16)
        def _(b):
            w = Rx[n, b]
            for g in range(4):
                dst[pl.ds(pl.multiple_of(b * 128 + 32 * g, 32), 32), :] = jnp.concatenate(
                    [w[:, 96 * g:96 * g + 96], jnp.full((32, 32), fill, bf)], axis=1)

    for n, dst, fill in ((0, Q, 0), (1, K, 0), (2, V, 1)):
        xq[n].wait_recv()
        unpack(n, dst, fill)
    Vt[...] = V[...].T
    xm.wait_recv()

    xb = []
    for half in (0, 1):
        @pl.loop(4 * half, 4 * half + 4)
        def _(j):
            attention(j, Q, K, Vt, ET, Oa, mixed, s_ref)
        if half == 0:
            ga.relay()
        for j in range(4 * half, 4 * half + 4):
            for i in (0, 1):
                b = 2 * j + i
                w = nn(main_places(M, b), mixed[128 * b:128 * b + 128, :]).astype(bf)
                B[:, 16 * i:16 * i + 16, 96 * j:96 * j + 96] = w[:, :96].reshape(16, 16, 96)
        cols = pl.ds(384 * half, 384)
        xb.append(Exchange(at, lambda t, cols=cols: B.at[t, :, cols], lambda t, cols=cols: RB.at[t, :, cols],
                           ss_b.at[half], rs_b.at[half]))
        xb[half].start()
    acc = jnp.zeros((512, 128), f32)
    for b in range(16):
        acc = acc + nn(extra_places(M, b), mixed[128 * b:128 * b + 128, :])
    B[:, :, 768:864] = acc[:, :96].astype(bf).reshape(16, 32, 96)
    B[:, :, 864:896] = jnp.zeros((16, 32, 32), bf)
    cols = pl.ds(768, 128)
    xb.append(Exchange(at, lambda t: B.at[t, :, cols], lambda t: RB.at[t, :, cols], ss_b.at[2], rs_b.at[2]))
    xb[2].start()
    RB[at.s] = B[at.s]
    ga.rest()
    xq[3].wait_recv()
    unpack(3, G, 0)

    for part in range(3):
        xb[part].wait_recv()
        for j in range(4 * part, min(4 * part + 4, 9)):
            rows[32 * j:32 * j + 32, :] = jnp.concatenate(
                [RB[h, :, 96 * j:96 * j + 96] for h in range(16)], axis=1)
    ga.far()
    for kk in range(4):
        ga.other(kk)
    for e in [xm, xs, xe] + xq + xb:
        e.wait_send()
    ga.wait_send()


def expert(rows, SA, wg, wu, wd, own_sum, grad_down, RA, ACT, DG, PT, SR, SS, RR,
           ss_g, rs_g, ss_s, rs_s, ss_r, rs_r):
    at = Place()
    greet(dp_peers(at))
    RA[at.dp] = rows[...]
    greeted(4)
    ga = Gather(at, RA, ss_g, rs_g)
    ga.own_out()

    def chunk(c):
        X = RA[c]
        Gr = SA[c]
        for f in range(2):
            fs = slice(256 * f, 256 * f + 256)
            gate = nn(X, wg[:, fs])
            up = nn(X, wu[:, fs])
            dact = nt(Gr, wd[fs, :])
            sig = 1.0 / (1.0 + jnp.exp(-gate))
            silu = gate * sig
            ACT[c, :, fs] = (silu * up).astype(bf)
            DG[:, 256 * f:256 * f + 256] = (dact * up * (sig * (1.0 + gate * (1.0 - sig)))).astype(bf)
            DG[:, 512 + 256 * f:768 + 256 * f] = (dact * silu).astype(bf)
        for n in range(3):
            ns = slice(512 * n, 512 * n + 512)
            PT[c, :, ns] = (nt(DG[:, :512], wg[ns, :]) + nt(DG[:, 512:], wu[ns, :])).astype(bf)

    def sib(k):
        return rcopy(PT.at[at.pair(k)], SR.at[k], ss_s.at[k], rs_s.at[k], (at.pair(0), at.s))

    def out(k):
        return rcopy(SS.at[k], RR.at[k], ss_r.at[k], rs_r.at[k], (at.clip(k), at.s))

    def send(k):
        sib(k).wait_recv()
        SS[k] = (PT[at.clip(k)].astype(f32) + SR[k].astype(f32)).astype(bf)
        if k:
            out(k).start()

    def work(k):
        chunk(at.pair(k))
        sib(k).start()
        chunk(at.clip(k))

    ga.other(0)
    work(0)
    ga.relay()
    ga.rest()
    send(0)
    ga.other(1)
    work(1)
    send(1)
    ga.far()
    ga.other(3)
    work(3)
    send(3)
    ga.other(2)
    work(2)
    send(2)
    for n in range(3):
        ns = slice(512 * n, 512 * n + 512)
        grad_down[:, ns] = tn(ACT[...].reshape(2304, 512), SA[:, :, ns].reshape(2304, 512)).astype(bf)
    total = SS[0].astype(f32)
    for k in (1, 3, 2):
        out(k).wait_recv()
        total = total + RR[k].astype(f32)
    own_sum[...] = total.astype(bf)
    for k in range(4):
        sib(k).wait_send()
        if k:
            out(k).wait_send()
    ga.wait_send()


def attention_back(j, dO, V, Kt, ET, Oa, dST, dOs, dQ):
    CH = 512
    q0 = pl.multiple_of(j * 256, 256)
    d = dO[pl.ds(q0, 256), :96].astype(f32)
    oa = Oa[pl.ds(q0, 256), :]
    linv = oa[:, 96:97]
    delta = -jnp.sum(d * oa[:, :96], axis=1, keepdims=True)
    hi = delta.astype(bf)
    r = delta - hi.astype(f32)
    mid = r.astype(bf)
    lo = (r - mid.astype(f32)).astype(bf)
    daug = jnp.concatenate([d.astype(bf), hi, mid, lo, jnp.zeros((256, 29), bf)], axis=1)
    dOs[pl.ds(q0, 256), :] = jnp.concatenate([(d * linv).astype(bf), jnp.zeros((256, 32), bf)], axis=1)
    for c in range(2048 // CH):
        dp = nt(V[c * CH:(c + 1) * CH, :], daug).astype(bf)
        dST[c * CH:(c + 1) * CH, pl.ds(q0, 256)] = ET[c * CH:(c + 1) * CH, pl.ds(q0, 256)] * dp
    dqt = nn(Kt[...], dST[:, pl.ds(q0, 256)])
    dQ[pl.ds(q0, 256), :] = (dqt.T * (linv * SC)).astype(bf)


def finish(total, Q, K, V, G, ET, Oa, M, gq, gk, gv,
           B, RB, dO, Kt, dST, dOs, Qs, dX, So, Ro, ss_b, rs_b, ss_o, rs_o):
    at = Place()
    greet(seq_peers(at))
    xb = []
    for part in range(3):
        cols = pl.ds(384 * part, 384 if part < 2 else 128)
        xb.append(Exchange(at, lambda t, cols=cols: B.at[t, :, cols], lambda t, cols=cols: RB.at[t, :, cols],
                           ss_b.at[part], rs_b.at[part]))
    for part in range(3):
        for h in range(16):
            parts = [total[32 * j:32 * j + 32, 96 * h:96 * h + 96] for j in range(4 * part, min(4 * part + 4, 9))]
            if part == 2:
                parts.append(jnp.zeros((32, 32), bf))
            B[h, :, 384 * part:384 * part + (384 if part < 2 else 128)] = jnp.concatenate(parts, axis=1)
        if part == 0:
            greeted(15)
        xb[part].start()
    RB[at.s] = B[at.s]
    Kt[...] = K[...].T
    Qs[...] = (Q[...].astype(f32) * (Oa[:, 96:97] * SC)).astype(bf)
    xb[2].wait_recv()
    extra = RB[:, :, 768:896].reshape(512, 128)
    for part in range(2):
        xb[part].wait_recv()
        for j in range(4 * part, 4 * part + 4):
            for i in (0, 1):
                b = 2 * j + i
                w = RB[:, 16 * i:16 * i + 16, 96 * j:96 * j + 96].reshape(256, 96)
                t = slice(128 * b, 128 * b + 128)
                dm = tn(main_places(M, b), w) + tn(extra_places(M, b), extra)[:, :96] + G[t, :96].astype(f32)
                dO[t, :96] = dm.astype(bf)

    xo = [Exchange(at, lambda t, n=n: So.at[n, t], lambda t, n=n: Ro.at[n, t], ss_o.at[n], rs_o.at[n])
          for n in range(3)]

    def pack(n):
        @pl.loop(0, 16)
        def _(b):
            So[n, b] = jnp.concatenate(
                [dX[pl.ds(pl.multiple_of(b * 128 + 32 * g, 32), 32), :96] for g in range(4)], axis=1)
        Ro[n, at.s] = So[n, at.s]
        xo[n].start()

    @pl.loop(0, 8)
    def _(j):
        attention_back(j, dO, V, Kt, ET, Oa, dST, dOs, dX)
    pack(0)
    for n, a, b in ((1, dST, Qs), (2, ET, dOs)):
        @pl.loop(0, 4)
        def _(i):
            r = pl.ds(pl.multiple_of(i * 512, 512), 512)
            dX[r, :] = nn(a[r, :], b[...]).astype(bf)
        pack(n)
    for n, dst in enumerate((gq, gk, gv)):
        xo[n].wait_recv()
        for g in range(4):
            dst[32 * g:32 * g + 32, :] = jnp.concatenate(
                [Ro[n, h, :, 96 * g:96 * g + 96] for h in range(16)], axis=1)
    for e in xb + xo:
        e.wait_send()


def call(kernel, outs, scratch, cid, *args):
    return pl.pallas_call(
        kernel,
        out_shape=[jax.ShapeDtypeStruct(s, d) for s, d in outs],
        scratch_shapes=scratch,
        name=kernel.__name__,
        compiler_params=pltpu.CompilerParams(collective_id=cid, has_side_effects=True, vmem_limit_bytes=VLIM),
    )(*args)


def vm(*shape, dtype=bf):
    return pltpu.VMEM(shape, dtype)


def dma(*shape):
    return pltpu.SemaphoreType.DMA(shape)


def run_front(query, key_in, value, grad_out, expert_ids, gate_weights):
    ids = expert_ids[0].astype(f32).T
    meta = jnp.concatenate([ids, gate_weights[0].T, jnp.zeros((4, 128), f32)], axis=0)
    return call(
        front,
        [((2048, 128), bf)] * 4 + [((2048, 2048), bf), ((2048, 128), f32), ((16, 8, 128), f32),
                                   ((288, 1536), bf), ((8, 288, 1536), bf)],
        [vm(4, 16, 32, 384), vm(4, 16, 32, 384), vm(8, 128, dtype=f32), vm(16, 16, 1536), vm(16, 16, 1536),
         vm(16, 32, 128), vm(16, 32, 128), vm(16, 32, 896), vm(16, 32, 896), vm(128, 2048), vm(2048, 128),
         vm(2048, 256, dtype=f32)]
        + [dma(4, 16)] * 2 + [dma(16)] * 6 + [dma(3, 16)] * 2 + [dma(14)] * 2,
        0, query[0], key_in[0], value[0], grad_out[0], meta)


def per_device(query, key_in, value, grad_out, expert_ids, gate_weights, w_gate, w_up, w_down):
    Q, K, V, G, ET, Oa, M, rows, SA = run_front(query, key_in, value, grad_out, expert_ids, gate_weights)
    total, grad_down = call(
        expert,
        [((288, 1536), bf), ((512, 1536), bf)],
        [vm(8, 288, 1536), vm(8, 288, 512), vm(288, 1024), vm(8, 288, 1536), vm(4, 288, 1536), vm(4, 288, 1536),
         vm(4, 288, 1536)] + [dma(14)] * 2 + [dma(4)] * 4,
        1, rows, SA, w_gate[0], w_up[0], w_down[0])
    gq, gk, gv = call(
        finish,
        [((128, 1536), bf)] * 3,
        [vm(16, 32, 896), vm(16, 32, 896), vm(2048, 128), vm(128, 2048), vm(2048, 2048), vm(2048, 128),
         vm(2048, 128), vm(2048, 128), vm(3, 16, 32, 384), vm(3, 16, 32, 384)]
        + [dma(3, 16)] * 4,
        2, total, Q, K, V, G, ET, Oa, M)
    return (gq[None], gk[None], gv[None], grad_down[None])


def solution(mesh):
    seq = P("dp", "seq", None)
    return jax.shard_map(
        per_device,
        mesh=mesh,
        in_specs=(seq,) * 6 + (P("seq", None, "dp"), P("seq", None, "dp"), P("seq", "dp", None)),
        out_specs=(seq, seq, seq, P("seq", "dp", None)),
        check_vma=False,
    )
```

time: 540 us -> 218 us (0.40); the launches traced: 530 us -> 217 us
  Pallas kernels: 0 us -> 208 us
  other arithmetic: 111 us -> 2.02 us
  waiting for transfers between devices: 97.8 us -> 0 us
  matrix products: 95.4 us -> 0 us
  local copies, waits for them, and re-layouts: 101 us -> 6.64 us
  blocking collectives: 55.3 us -> 0 us
  starting transfers between devices: 55.3 us -> 0 us
  between operations: 14.9 us -> 0.67 us
    pallas_call x0 -> x3, Pallas kernels: none -> 208 us  [call(): pl.pallas_call(kernel, out_shape=[jax.ShapeDtypeStruct(s, d) for s, d in...]
    dot_general x14 -> x0, matrix products: 95.4 us -> none  [the longest x1 12.3 us: slice_partial(): lax.dot_general(joined, weights, (((1,), (1,)), ((), ())), preferred_elem...]
    unnamed x8 -> x0, other arithmetic: 91.1 us -> none
    reduce_scatter x1 -> x0, waiting for transfers between devices: 56.4 us -> none  [per_device(): lax.psum_scatter(partial_value.astype(jnp.bfloat16), 'dp', scatter_dimens...]
    all_to_all x3 -> x0, blocking collectives: 55.3 us -> none  [the longest x1 25.2 us: per_device(): lax.all_to_all(send_grad, 'seq', split_axis=0, concat_axis=0, tiled=True)]
    all_to_all x8 -> x0, starting transfers between devices: 55.2 us -> none  [the longest x1 7.66 us: per_device(): lax.all_to_all(join_heads(dq), 'seq', split_axis=1, concat_axis=2, tiled=...]
    all_to_all x8 -> x0, waiting for transfers between devices: 30.1 us -> none  [the longest x1 18 us: per_device(): lax.all_to_all(summed, 'seq', split_axis=0, concat_axis=0, tiled=True)]
    reshape x6 -> x0, local copies, waits for them, and re-layouts: 26 us -> none  [the longest x1 11.4 us: per_device(): all_in.reshape(total_rows, width)]
  transfers between devices with their start and end apart: 11 -> 0, of which waited for: 5 -> 0; matrix products, arithmetic and copies ran while one was open for 36% -> 0% of each run, Pallas kernels for 0% -> 0%
where the time goes in v1:
time: 218 us; the launch traced here: 217 us
  Pallas kernels  208 us (95%)
  local copies, waits for them, and re-layouts  6.64 us (3%)
    pallas_call x3, Pallas kernels, call(): pl.pallas_call(kernel, out_shape=[jax.ShapeDtypeStruct(s, d) for s, d in...  208 us
    unnamed x6, local copies, waits for them, and re-layouts  6.56 us

profile of v1, /device:TPU:10, one launch (start us, length us, event | category | flops | bytes accessed | tf_op | source)
XLA Modules:
  0.0 217.2 jit_solution(11228618772553162413)
XLA Ops:
  0.6 0.1 pad.2.clone
  0.7 0.7 convert_bitcast_fusion
  1.4 1.3 maximum_maximum_fusion.meta
  2.7 71.7 %front.1 = (bf16[2048,128]{1,0:T(8,128)(2,1)}, bf16[2048,128]{1,0:T(8,128)(2,1)}, bf16[2048,128]{1,0:T(8,128)(2,1)}, bf16[2048,128]{1,0:T(8,128)(2,1)}, bf16[204...) custom-call(bf16[128,1536]{1,0:T(8,128)(2,1)} %bitcast.25, ...), custom_call_target="tpu_custom_call" | custom-call | tf_op jit(solution)/shard_map/front/pallas_call | solution.py:482
  74.5 86.3 %expert.1 = (bf16[288,1536]{1,0:T(8,128)(2,1)}, bf16[512,1536]{1,0:T(8,128)(2,1)}) custom-call(bf16[288,1536]{1,0:T(8,128)(2,1)} %get-tuple-element.18.rows, bf16[8,288,1536]{2,1,0:T(8,128)(2,1)} %get-tuple-element.19.SA, bf16[1536,512]{1,0:T(8,128)(2,1)} %bitcast.18, bf16[1536,512]{1,0:T(8,128)(2,1)} %bitcast.19, bf16[512,1536]{1,0:T(8,128)(2,1)} %bitcast.20), custom_call_target="tpu_custom_call" | custom-call | tf_op jit(solution)/shard_map/expert/pallas_call | solution.py:482
  160.8 49.9 %finish.1 = (bf16[128,1536]{1,0:T(8,128)(2,1)}, bf16[128,1536]{1,0:T(8,128)(2,1)}, bf16[128,1536]{1,0:T(8,128)(2,1)}) custom-call(bf16[288,1536]{1,0:T(8,128)(2,1)} %get-tuple-element.20.total, bf16[2048,128]{1,0:T(8,128)(2,1)} %get-tuple-element.21.Q, bf16[2048,128]{1,0:T(8,128)(2,1)} %get-tuple-element.22.K, bf16[2048,128]{1,0:T(8,128)(2,1)} %get-tuple-element.23.V, ...), custom_call_target="tpu_custom_call" | custom-call | tf_op jit(solution)/shard_map/finish/pallas_call | solution.py:482
  210.7 0.0 copy-start
  210.7 1.9 copy.17
  212.6 1.8 copy.18
  214.3 1.8 copy.19
  216.1 0.0 copy-done
  216.1 1.1 copy.20
  (1 shorter events, 0.0 us)
Async XLA Ops:
  210.7 5.4 %copy-start = (bf16[512,1536]{1,0:T(8,128)(2,1)S(1)}, bf16[512,1536]{1,0:T(8,128)(2,1)}, u32[]{:S(2)}) copy-start(bf16[512,1536]{1,0:T(8,128)(2,1)} %get-tuple-element.31) | copy-start | bytes 4718596
